TPU v7x, 256 devices: a whole 4x4x8 slice. The times are simulated.
256 devices in a mesh: row: 8 (over y_lo, x), col: 32 (over z, y_hi, core).
Axes of the slice: x: 4, y: 4 (y_hi: 2, y_lo: 2; y = y_hi * 2 + y_lo), z: 8, core: 2. Of those that a mesh axis runs over, the one named last changes fastest.
Arguments:
- iterate: bfloat16 [3584, 16384], P('row', 'col'), may hold values from -0.0390625 to 0.0390625
Outputs:
- update: bfloat16 [3584, 16384], P('row', 'col')
All inputs are finite; a program needn't handle non-finite values.
Results may differ from a plain program's by a relative error of at most 0.0087.
Values may be sent and summed in bfloat16 or wider, within the bound.
A program may use at most 64 MiB of HBM per device.

v0:
```python
import math

import jax
import jax.numpy as jnp
from jax import lax
from jax.sharding import PartitionSpec as P

N = 16384


def spread(array, axis, root):
    mine = lax.axis_index(axis) == root
    return lax.psum(jnp.where(mine, array, jnp.zeros_like(array)), axis)


def on_device(iterate):
    n_row = lax.axis_size("row")
    n_col = lax.axis_size("col")
    panel = lax.all_gather(iterate, "row", axis=0, tiled=True)
    total_rows = panel.shape[0]
    width = total_rows // n_col
    col_index = lax.axis_index("col")
    partial_value = lax.dot_general(
        iterate, panel, (((1,), (1,)), ((), ())), preferred_element_type=jnp.float32
    )
    gram_row = lax.psum(partial_value, "col").astype(jnp.bfloat16)
    own_cols = lax.dynamic_slice_in_dim(gram_row, col_index * width, width, 1)
    per_block = n_col // n_row
    offset = col_index % per_block * width
    local_rows = lax.dynamic_slice_in_dim(gram_row, offset, width, 0)
    mirrored = spread(local_rows, "row", col_index // per_block)
    square = lax.dot_general(
        gram_row, mirrored, (((1,), (1,)), ((), ())), preferred_element_type=jnp.float32
    )
    poly = (-4.775 * own_cols.astype(jnp.float32) + 2.0315 * square).astype(jnp.bfloat16)
    product = jnp.dot(
        lax.all_gather(poly, "col", axis=1, tiled=True), panel, preferred_element_type=jnp.float32
    )
    scale = math.sqrt(N)
    return ((3.4445 * iterate.astype(jnp.float32) + product) * scale).astype(jnp.bfloat16)


def solution(mesh):
    in_specs = (P("row", "col"),)
    out_specs = P("row", "col")
    return jax.shard_map(
        on_device, mesh=mesh, in_specs=in_specs, out_specs=out_specs, check_vma=False
    )
```

profile of v0, /device:TPU:1, one launch (start us, length us, event | category | flops | bytes accessed | tf_op | source)
XLA Modules:
  0.0 419.1 jit_solution(12727327061314107934)
XLA Ops:
  6.5 0.0 all-gather.3.cloned.1.call-start
  6.5 0.7 all-gather.3.cloned.1.call-update
  7.3 0.0 all-reduce.3.cloned.1.call-start
  7.3 55.8 %all-gather.3.cloned.1.call-done = bf16[3584,512]{1,0:T(8,128)(2,1)} async-done(((bf16[448,512]{1,0:T(8,128)(2,1)}), bf16[3584,512]{1,0:T(8,128)(2,1)}) %all-gather.3.cloned.1.call-update) | async-done | bytes 3670032 | tf_op jit(solution)/shard_map/all_gather | solution.py:19
  63.2 6.8 %fusion.4 = f32[448,3584]{1,0:T(8,128)} fusion(bf16[448,512]{1,0:T(8,128)(2,1)} %param.1, bf16[3584,512]{1,0:T(8,128)(2,1)} %all-gather.3.cloned.1.call-done), kind=kOutput, calls=%fused_computation.7 | convolution fusion | flops 1644167168 | bytes 10551296 | tf_op jit(solution)/shard_map/dot_general | solution.py:23
  69.9 161.4 %all-reduce.4 = bf16[448,3584]{1,0:T(8,128)(2,1)S(1)} all-reduce(f32[448,3584]{1,0:T(8,128)} %fusion.4), channel_id=1, replica_groups=mesh['row'=8,'col'=32] {'col'}, use_global_device_ids=true, to_apply=%region_0.0 | all-reduce | flops 1605632 | bytes 9633792 | tf_op jit(solution)/shard_map/psum | solution.py:26
  231.4 1.0 dynamic-slice_select_fusion
  232.4 0.0 all-reduce.3.cloned.1.call-update
  232.4 0.0 all-gather.5.cloned.1.call-start
  232.5 81.2 %all-reduce.3.cloned.1.call-done = bf16[112,3584]{1,0:T(8,128)(2,1)} async-done(((bf16[112,3584]{1,0:T(8,128)(2,1)}), bf16[112,3584]{1,0:T(8,128)(2,1)}) %all-reduce.3.cloned.1.call-update) | async-done | bytes 802832 | tf_op jit(solution)/shard_map/psum | solution.py:13
  313.7 2.1 fusion.3
  315.8 0.8 copy.2
  316.5 0.0 all-gather.5.cloned.1.call-update
  316.6 90.3 %all-gather.5.cloned.1.call-done = bf16[448,3584]{0,1:T(8,128)(2,1)} async-done(((bf16[448,112]{0,1:T(8,128)(2,1)}), bf16[448,3584]{0,1:T(8,128)(2,1)}) %all-gather.5.cloned.1.call-update) | async-done | bytes 3211280 | tf_op jit(solution)/shard_map/all_gather | solution.py:37
  406.8 5.8 %fusion.1 = bf16[448,512]{1,0:T(8,128)(2,1)} fusion(bf16[448,3584]{0,1:T(8,128)(2,1)} %all-gather.5.cloned.1.call-done, bf16[3584,512]{1,0:T(8,128)(2,1)} %all-gather.3.cloned.1.call-done, bf16[448,512]{1,0:T(8,128)(2,1)} %param.1), kind=kOutput, calls=%fused_computation.2 | convolution fusion | flops 1645314048 | bytes 7798784 | tf_op jit(solution)/shard_map/dot_general | solution.py:36
Async XLA Ops:
  6.5 56.6 %all-gather.3.cloned.1.call-start = ((), (), s32[]{:S(2)}) async-start(), calls=%async_computation | async-start | bytes 4128768 | tf_op jit(solution)/shard_map/all_gather | solution.py:19
  7.3 306.4 %all-reduce.3.cloned.1.call-start = ((), (), s32[]{:S(2)}) async-start(), calls=%async_computation.1 | async-start | bytes 1605632 | tf_op jit(solution)/shard_map/psum | solution.py:13
  232.4 174.4 %all-gather.5.cloned.1.call-start = ((), (), s32[]{:S(2)}) async-start(), calls=%async_computation.2 | async-start | bytes 3784704 | tf_op jit(solution)/shard_map/all_gather | solution.py:37
Sparse Core Ops, SparseCore 0:
  9.1 53.9 all-gather.2
  232.6 81.0 all-reduce.2
  316.8 89.9 all-gather.4
where the time goes:
time: 419 us
  waiting for transfers between devices  228 us (54%)
  blocking collectives  161 us (38%)
  matrix products  14.7 us (4%)
  between operations  13.2 us (3%)
    psum x1, blocking collectives, on_device(): gram_row = lax.psum(partial_value, 'col').astype(jnp.bfloat16)  161 us
    all_gather x1, waiting for transfers between devices, on_device(): lax.all_gather(poly, 'col', axis=1, tiled=True)  90.3 us
    psum x1, waiting for transfers between devices, spread(): return lax.psum(jnp.where(mine, array, jnp.zeros_like(array)), axis)  81.2 us
    all_gather x1, waiting for transfers between devices, on_device(): panel = lax.all_gather(iterate, 'row', axis=0, tiled=True)  55.8 us
  transfers between devices with their start and end apart: 3, of which 3 were waited for; matrix products, arithmetic and copies ran while one was open for 0% of the time, Pallas kernels for 0%

commit v1 on v0

v1 whole, which is shorter than its diff:
```python
import math

import jax
import jax.numpy as jnp
from jax import lax
from jax.experimental import pallas as pl
from jax.experimental.pallas import tpu as pltpu
from jax.sharding import PartitionSpec as P

N = 16384
B = 448
W = 512
NX = 4
HALF = NX * B
NQ = 2
Q = W // NQ
HW = HALF // 2
CH = B // 4
SH = 64
F32 = jnp.float32
BF16 = jnp.bfloat16
NT = (((1,), (1,)), ((), ()))
PIECES = ((0, 256), (256, 256), (512, 256), (768, 128))


def kernel(
    x_ref, out_ref, panel, ypanel, tsend, town, ybuf, zsrc, zbuf, agbuf, poly,
    part, rbuf, yown, loc_sem, xs, xr, cs, cr, ls, lr, ys, yr, zs, zr, gs, gr, hs, hr,
    ps, pr,
):
    row = lax.axis_index("row")
    col = lax.axis_index("col")
    x = row % 4
    low = row // 4
    core = col % 2
    high = (col // 2) % 2
    z = col // 4

    def at(x_=None, low_=None, z_=None, high_=None, core_=None):
        x_ = x if x_ is None else x_
        low_ = low if low_ is None else low_
        z_ = z if z_ is None else z_
        high_ = high if high_ is None else high_
        core_ = core if core_ is None else core_
        return (low_ * 4 + x_, z_ * 4 + high_ * 2 + core_)

    def remote(src, dst, send, recv, dev):
        return pltpu.make_async_remote_copy(
            src_ref=src, dst_ref=dst, send_sem=send, recv_sem=recv,
            device_id=dev, device_id_type=pl.DeviceIdType.MESH,
        )

    up = at(x_=(x + 1) % 4)
    down = at(x_=(x + 3) % 4)
    twin = at(core_=1 - core)
    across = at(high_=1 - high)

    barrier = pltpu.get_barrier_semaphore()
    peers = [up, down, twin, across]
    peers += [at(low_=1 - low, core_=k) for k in range(2)]
    peers += [at(z_=(z + d) % 8) for d in range(1, 8)]
    for dev in peers:
        pl.semaphore_signal(barrier, inc=1, device_id=dev, device_id_type=pl.DeviceIdType.MESH)
    pl.semaphore_wait(barrier, len(peers))

    h = B // 2

    def gather(src, slot, n):
        own = src
        a, b = pl.ds(0, h), pl.ds(h, h)
        first = [
            remote(own.at[a], slot(core, B, h), xs.at[n, 0], xr.at[n, 0], down),
            remote(own.at[b], slot(core, 3 * B + h, h), xs.at[n, 1], xr.at[n, 1], up),
            remote(own.at[b], slot(core, B + h, h), xs.at[n, 2], xr.at[n, 2], down),
            remote(own.at[a], slot(core, 3 * B, h), xs.at[n, 3], xr.at[n, 3], up),
        ]
        passed = [
            remote(slot(core, B, h), slot(core, 2 * B, h), xs.at[n, 4], xr.at[n, 4], down),
            remote(slot(core, 3 * B + h, h), slot(core, 2 * B + h, h), xs.at[n, 5], xr.at[n, 5], up),
        ]
        places = [B, 3 * B + h, B + h, 3 * B, 2 * B, 2 * B + h]
        cross = [
            remote(slot(core, p, h), slot(core, p, h), cs.at[n, k], cr.at[n, k], twin)
            for k, p in enumerate(places)
        ]
        cross.append(remote(own, slot(core, 0, B), cs.at[n, 6], cr.at[n, 6], twin))

        def start():
            for c in first:
                c.start()
            cross[6].start()

        def relay():
            for k in range(6):
                (first + passed)[k].wait_recv()
                if k < 2:
                    passed[k].start()
                cross[k].start()

        def done():
            for c in cross:
                c.wait_recv()

        def close():
            for c in first + passed + cross:
                c.wait_send()

        return start, relay, done, close

    def xslot(c, at_row, rows):
        return panel.at[c, pl.ds(at_row, rows)]

    start, relay, done, close = gather(x_ref, xslot, 0)
    start()
    other = remote(
        x_ref, panel.at[core, pl.ds(HALF, B)], ls.at[0], lr.at[core], at(low_=1 - low, core_=1)
    )
    other.start()
    keep = pltpu.make_async_copy(x_ref, panel.at[core, pl.ds(0, B)], loc_sem)
    keep.start()
    relay()
    keep.wait()
    done()

    @pl.when(core == 1)
    def _():
        for k in range(2):
            remote(
                x_ref, panel.at[k, pl.ds(HALF, B)], ls.at[0], lr.at[k], at(low_=1 - low, core_=1)
            ).wait_recv()

    left = pl.multiple_of(core * HALF, 64)

    def gram(base, at_col, size):
        total = None
        for c in range(2):
            rows = pl.ds(pl.multiple_of(base + at_col, 64), size)
            term = lax.dot_general(
                panel[c, pl.ds(left, B), :], panel[c, rows, :], NT, preferred_element_type=F32
            )
            total = term if total is None else total + term
        return total

    for at_col, size in PIECES:
        tsend[:, at_col : at_col + size] = gram((1 - high) * HW, at_col, size).astype(BF16)
    i0 = z // 2
    ysend = []
    for s in range(4):
        rows = pl.ds(pl.multiple_of((i0 + s) % 4 * CH, 16), CH)
        ysend.append(remote(tsend.at[rows], ybuf.at[rows], ys.at[s], yr.at[s], across))
        ysend[s].start()
    for at_col, size in PIECES:
        town[:, at_col : at_col + size] = gram(high * HW, at_col, size)

    par = z % 2
    zsend = []
    for s in range(4):
        chunk = (i0 + s) % 4
        rows = pl.ds(pl.multiple_of(chunk * CH, 16), CH)
        ysend[s].wait_recv()
        zsrc[rows, :] = (town[rows, :] + ybuf[rows, :].astype(F32)).astype(BF16)
        if s == 0:
            odd = 1 - par
            piece = pl.ds(pl.multiple_of(chunk * CH + odd * (CH - SH), 16), SH)
            zsend.append(
                remote(zsrc.at[piece], zbuf.at[0], zs.at[0], zr.at[0], at(z_=2 * chunk + odd))
            )
            zsend[-1].start()
        else:
            for odd in range(2):
                piece = pl.ds(pl.multiple_of(chunk * CH + odd * (CH - SH), 16), SH)
                k = 2 * s - 1 + par
                zsend.append(
                    remote(
                        zsrc.at[piece], zbuf.at[k], zs.at[2 * s - 1 + odd], zr.at[k],
                        at(z_=2 * chunk + odd),
                    )
                )
                zsend[-1].start()
    mine = pl.ds(pl.multiple_of(i0 * CH + par * (CH - SH), 16), SH)
    total = zsrc[mine, :].astype(F32)
    for k in range(7):
        remote(zbuf.at[k], zbuf.at[k], zs.at[k], zr.at[k], at(z_=(z + 1) % 8)).wait_recv()
        total = total + zbuf[k].astype(F32)
    agbuf[0, 7] = total.astype(BF16)

    gsend = []
    for s in range(4):
        chunk = (i0 + s) % 4
        for odd in range(2) if s else (1 - par,):
            k = 2 * s - 1 + par if s else 0
            gsend.append(
                remote(
                    agbuf.at[0, 7], agbuf.at[0, k], gs.at[len(gsend)], gr.at[k],
                    at(z_=2 * chunk + odd),
                )
            )
            gsend[-1].start()
    hsend = [remote(agbuf.at[0, k], agbuf.at[1, k], hs.at[k], hr.at[k], across) for k in range(8)]
    hsend[7].start()

    def first_row(k):
        if k == 7:
            return i0 * CH + par * (CH - SH)
        if k == 0:
            return i0 * CH + (1 - par) * (CH - SH)
        s, odd = (k + 1) // 2, (k + 1) % 2
        return (i0 + 4 - s) % 4 * CH + odd * (CH - SH)

    def place(side, k):
        rows = pl.ds(pl.multiple_of(first_row(k), 16), SH)
        half = high if side == 0 else 1 - high
        poly[rows, pl.ds(pl.multiple_of(half * HW, 128), HW)] = agbuf[side, k]

    place(0, 7)
    for k in range(7):
        remote(agbuf.at[0, k], agbuf.at[0, k], gs.at[k], gr.at[k], at(z_=(z + 1) % 8)).wait_recv()
        hsend[k].start()
        place(0, k)
    for k in (7, 0, 1, 2, 3, 4, 5, 6):
        hsend[k].wait_recv()
        place(1, k)

    def send_partial(n, q):
        one = remote(
            part.at[n, q, 1], rbuf.at[n, q, core], ps.at[n, q, 1], pr.at[n, q, core],
            (row + core * (4 - 8 * low), z * 4 + high * 2 + 1),
        )
        one.start()

        @pl.when(core == 1)
        def _():
            remote(
                part.at[n, q, 0], rbuf.at[n, q, 1], ps.at[n, q, 0], pr.at[n, q, 1],
                at(low_=1 - low, core_=0),
            ).start()

    def reduced(n, q):
        remote(
            part.at[n, q, 1], rbuf.at[n, q, 1], ps.at[n, q, 1], pr.at[n, q, 1], twin
        ).wait_recv()

        @pl.when(core == 1)
        def _():
            remote(
                part.at[n, q, 0], rbuf.at[n, q, 0], ps.at[n, q, 0], pr.at[n, q, 0], twin
            ).wait_recv()

        @pl.when(core == 0)
        def _():
            rbuf[n, q, 0] = part[n, q, 0]

        return rbuf[n, q, 0].astype(F32) + rbuf[n, q, 1].astype(F32)

    def partial_close(n, q):
        remote(
            part.at[n, q, 1], rbuf.at[n, q, 1], ps.at[n, q, 1], pr.at[n, q, 1], twin
        ).wait_send()

        @pl.when(core == 1)
        def _():
            remote(
                part.at[n, q, 0], rbuf.at[n, q, 0], ps.at[n, q, 0], pr.at[n, q, 0], twin
            ).wait_send()

    for q in range(NQ):
        for c in range(2):
            term = jnp.dot(
                poly[...], panel[c, pl.ds(0, HALF), q * Q : (q + 1) * Q],
                preferred_element_type=F32,
            )
            yown[q, c] = term
            part[0, q, c] = term.astype(BF16)
        send_partial(0, q)
    rings = []
    for q in range(NQ):
        ypanel[q, core, pl.ds(0, B)] = reduced(0, q).astype(BF16)

        def yslot(c, at_row, rows, q=q):
            return ypanel.at[q, c, pl.ds(at_row, rows)]

        rings.append(gather(ypanel.at[q, core, pl.ds(0, B)], yslot, 1 + q))
        rings[q][0]()
    for q in range(NQ):
        rings[q][1]()
    for q in range(NQ):
        rings[q][2]()
        for c in range(2):
            term = jnp.dot(poly[...], ypanel[q, c], preferred_element_type=F32)
            part[1, q, c] = (2.0315 * term - 4.775 * yown[q, c]).astype(BF16)
        send_partial(1, q)
    scale = math.sqrt(N)
    for q in range(NQ):
        cols = slice(q * Q, (q + 1) * Q)
        total = 3.4445 * x_ref[:, cols].astype(F32) + reduced(1, q)
        out_ref[:, cols] = (total * scale).astype(BF16)

    close()
    other.wait_send()
    for c in ysend + zsend + gsend + hsend:
        c.wait_send()
    for q in range(NQ):
        rings[q][3]()
        for n in range(2):
            partial_close(n, q)


def on_device(iterate):
    dma = pltpu.SemaphoreType.DMA
    return pl.pallas_call(
        kernel,
        out_shape=jax.ShapeDtypeStruct((B, W), BF16),
        in_specs=[pl.BlockSpec(memory_space=pltpu.VMEM)],
        out_specs=pl.BlockSpec(memory_space=pltpu.VMEM),
        scratch_shapes=[
            pltpu.VMEM((2, HALF + B, W), BF16),
            pltpu.VMEM((NQ, 2, HALF, Q), BF16),
            pltpu.VMEM((B, HW), BF16),
            pltpu.VMEM((B, HW), F32),
            pltpu.VMEM((B, HW), BF16),
            pltpu.VMEM((B, HW), BF16),
            pltpu.VMEM((7, SH, HW), BF16),
            pltpu.VMEM((2, 8, SH, HW), BF16),
            pltpu.VMEM((B, HALF), BF16),
            pltpu.VMEM((2, NQ, 2, B, Q), BF16),
            pltpu.VMEM((2, NQ, 2, B, Q), BF16),
            pltpu.VMEM((NQ, 2, B, Q), F32),
            dma,
            dma((1 + NQ, 6)), dma((1 + NQ, 6)),
            dma((1 + NQ, 7)), dma((1 + NQ, 7)),
            dma((1,)), dma((2,)),
            dma((4,)), dma((4,)),
            dma((7,)), dma((7,)),
            dma((7,)), dma((7,)),
            dma((8,)), dma((8,)),
            dma((2, NQ, 2)), dma((2, NQ, 2)),
        ],
        compiler_params=pltpu.CompilerParams(
            collective_id=0, has_side_effects=True, vmem_limit_bytes=56 * 2**20
        ),
    )(iterate)


def solution(mesh):
    in_specs = (P("row", "col"),)
    out_specs = P("row", "col")
    return jax.shard_map(
        on_device, mesh=mesh, in_specs=in_specs, out_specs=out_specs, check_vma=False
    )
```

time: 419 us -> 136 us (0.32)
  waiting for transfers between devices: 228 us -> 0 us
  blocking collectives: 161 us -> 0 us
  Pallas kernels: 0 us -> 133 us
  matrix products: 14.7 us -> 0 us
  between operations: 13.2 us -> 0.01 us
    psum x1 -> x0, blocking collectives: 161 us -> none  [on_device(): gram_row = lax.psum(partial_value, 'col').astype(jnp.bfloat16)]
    all_gather x2 -> x0, waiting for transfers between devices: 146 us -> none  [the longest x1 90.3 us: on_device(): lax.all_gather(poly, 'col', axis=1, tiled=True)]
    pallas_call x0 -> x1, Pallas kernels: none -> 133 us  [on_device(): pl.pallas_call(kernel, out_shape=jax.ShapeDtypeStruct((B, W), BF16), in_s...]
    psum x1 -> x0, waiting for transfers between devices: 81.2 us -> none  [spread(): return lax.psum(jnp.where(mine, array, jnp.zeros_like(array)), axis)]
    dot_general x3 -> x0, matrix products: 14.7 us -> none  [the longest x1 6.75 us: on_device(): lax.dot_general(iterate, panel, (((1,), (1,)), ((), ())), preferred_eleme...]
  transfers between devices with their start and end apart: 3 -> 0, of which waited for: 3 -> 0; matrix products, arithmetic and copies ran while one was open for 0% -> 0% of each run, Pallas kernels for 0% -> 0%
where the time goes in v1:
time: 136 us; the launch traced here: 134 us
  Pallas kernels  133 us (98%)
  local copies, waits for them, and re-layouts  1.82 us (1%)
    pallas_call x1, Pallas kernels, on_device(): pl.pallas_call(kernel, out_shape=jax.ShapeDtypeStruct((B, W), BF16), in_s...  133 us

profile of v1, /device:TPU:1, one launch (start us, length us, event | category | flops | bytes accessed | tf_op | source)
XLA Modules:
  0.0 134.5 jit_solution(15288592800359117061)
XLA Ops:
  0.0 132.7 %shard_map.17 = bf16[448,512]{1,0:T(8,128)(2,1)} custom-call(bf16[448,512]{1,0:T(8,128)(2,1)} %x_ref.1), custom_call_target="tpu_custom_call" | custom-call | tf_op jit(solution)/shard_map/pallas_call | solution.py:310
  132.7 1.8 %copy.3 = bf16[448,512]{1,0:T(8,128)(2,1)} copy(bf16[448,512]{1,0:T(8,128)(2,1)} %shard_map.17) | data formatting | bytes 917504

commit v2 on v1

v2 whole, which is shorter than its diff:
```python
import math

import jax
import jax.numpy as jnp
from jax import lax
from jax.experimental import pallas as pl
from jax.experimental.pallas import tpu as pltpu
from jax.sharding import PartitionSpec as P

N = 16384
B = 448
W = 512
S = 512
NX = 4
NJ = 3
NQ = 2
Q = W // NQ
HB = B // 2
PR = HB // 2
PC = S // 4
F32 = jnp.float32
BF16 = jnp.bfloat16
NT = (((1,), (1,)), ((), ()))
MESH = pl.DeviceIdType.MESH


def kernel(
    x_ref, out_ref, panel, ypanel, tsend, town, ybuf, zsrc, zbuf, gsh, agbuf, poly, mbuf,
    part, rbuf, yown, loc_sem, xs, xr, cs, cr, ls, lr, ys, yr, zs, zr, gs, gr, hs, hr,
    ms, mr, ps, pr,
):
    row = lax.axis_index("row")
    col = lax.axis_index("col")
    x = row % 4
    low = row // 4
    core = col % 2
    high = (col // 2) % 2
    z = col // 4

    def at(x_=None, low_=None, z_=None, high_=None, core_=None):
        x_ = x if x_ is None else x_
        low_ = low if low_ is None else low_
        z_ = z if z_ is None else z_
        high_ = high if high_ is None else high_
        core_ = core if core_ is None else core_
        return (low_ * 4 + x_, z_ * 4 + high_ * 2 + core_)

    def remote(src, dst, send, recv, dev):
        return pltpu.make_async_remote_copy(
            src_ref=src, dst_ref=dst, send_sem=send, recv_sem=recv,
            device_id=dev, device_id_type=MESH,
        )

    pend = []
    up = at(x_=(x + 1) % 4)
    down = at(x_=(x + 3) % 4)
    twin = at(core_=1 - core)
    across = at(high_=1 - high)
    other_low = low + core * (1 - 2 * low)
    mirror_to = at(x_=(x + 1) % 4, low_=other_low)
    mirror_from = at(x_=(x + 3) % 4, low_=other_low)

    barrier = pltpu.get_barrier_semaphore()
    peers = [up, down, twin, across, mirror_to, mirror_from]
    peers += [at(low_=1 - low, core_=k) for k in range(2)]
    peers += [at(z_=(z + d) % 8) for d in range(1, 8)]
    for dev in peers:
        pl.semaphore_signal(barrier, inc=1, device_id=dev, device_id_type=MESH)
    for c in range(2):
        for j in range(NJ):
            panel[c, j * S + B : (j + 1) * S, :] = jnp.zeros((S - B, W), BF16)
    panel[0, 3 * S + B : 4 * S, :] = jnp.zeros((S - B, W), BF16)
    panel[1, 3 * S + B : 4 * S, :] = jnp.zeros((S - B, W), BF16)
    for q in range(NQ):
        for c in range(2):
            for j in range(NX):
                ypanel[q, c, j * S + B : (j + 1) * S, :] = jnp.zeros((S - B, Q), BF16)
    pl.semaphore_wait(barrier, len(peers))

    h = B // 2

    def gather(own, slot, n):
        a, b = pl.ds(0, h), pl.ds(h, h)
        direct = [
            remote(own.at[a], slot(core, S, h), xs.at[n, 0], xr.at[n, 0], down),
            remote(own.at[b], slot(core, 3 * S + h, h), xs.at[n, 1], xr.at[n, 1], up),
            remote(own.at[b], slot(core, S + h, h), xs.at[n, 2], xr.at[n, 2], down),
            remote(own.at[a], slot(core, 3 * S, h), xs.at[n, 3], xr.at[n, 3], up),
        ]
        passed = [
            remote(slot(core, S, h), slot(core, 2 * S, h), xs.at[n, 4], xr.at[n, 4], down),
            remote(slot(core, 3 * S + h, h), slot(core, 2 * S + h, h), xs.at[n, 5], xr.at[n, 5], up),
        ]
        moves = direct + passed
        places = [S, 3 * S + h, S + h, 3 * S, 2 * S, 2 * S + h]
        cross = [
            remote(slot(core, p, h), slot(core, p, h), cs.at[n, k], cr.at[n, k], twin)
            for k, p in enumerate(places)
        ]
        cross.append(remote(own, slot(core, 0, B), cs.at[n, 6], cr.at[n, 6], twin))

        def start():
            cross[6].start()
            for k in range(3):
                direct[k].start()

        def relay(k):
            moves[k].wait_recv()
            if k < 2:
                passed[k].start()
            if k == 1:
                direct[3].start()
            cross[k].start()

        def done(ks):
            for k in ks:
                cross[k].wait_recv()

        def close():
            for c in moves + cross:
                c.wait_send()

        return start, relay, done, close

    def xslot(c, at_row, rows):
        return panel.at[c, pl.ds(at_row, rows)]

    start, relay, done, close = gather(x_ref, xslot, 0)
    start()
    other = remote(
        x_ref, panel.at[core, pl.ds(NX * S, B)], ls.at[0], lr.at[core], at(low_=1 - low, core_=1)
    )
    other.start()
    keep = pltpu.make_async_copy(x_ref, panel.at[core, pl.ds(0, B)], loc_sem)
    keep.start()
    keep.wait()
    done([6])

    left = core * NX * S

    def gram(half, j):
        rows = pl.ds(pl.multiple_of(left + half * HB, 32), HB)
        total = None
        for c in range(2):
            term = lax.dot_general(
                panel[c, rows, :], panel[c, pl.ds(j * S, S), :], NT, preferred_element_type=F32
            )
            total = term if total is None else total + term
        return total

    ysend = [remote(tsend.at[j], ybuf.at[j], ys.at[j], yr.at[j], across) for j in range(NJ)]

    def make(j):
        tsend[j] = gram(1 - high, j).astype(BF16)
        ysend[j].start()
        town[j] = gram(high, j)

    zsend = [
        [
            remote(
                zsrc.at[j, (z + d) % 8], zbuf.at[j, d - 1], zs.at[j, d - 1], zr.at[j, d - 1],
                at(z_=(z + d) % 8),
            )
            for d in (1, 7, 2, 6, 3, 5, 4)
        ]
        for j in range(NJ)
    ]

    def scatter(j):
        ysend[j].wait_recv()
        for p in range(8):
            rows = slice(p % 2 * PR, (p % 2 + 1) * PR)
            cols = slice(p // 2 * PC, (p // 2 + 1) * PC)
            zsrc[j, p] = (town[j, rows, cols] + ybuf[j, rows, cols].astype(F32)).astype(BF16)
        for c in zsend[j]:
            c.start()

    gsend = [
        [
            remote(
                gsh.at[j], agbuf.at[high, j, z], gs.at[j, d - 1], gr.at[j, d - 1],
                at(z_=(z + d) % 8),
            )
            for d in (1, 7, 2, 6, 3, 5, 4)
        ]
        for j in range(NJ)
    ]

    def spread(j):
        total = zsrc[j, z].astype(F32)
        for c in zsend[j]:
            c.wait_recv()
        for k in range(7):
            total = total + zbuf[j, k].astype(F32)
        gsh[j] = total.astype(BF16)
        for c in gsend[j]:
            c.start()
        agbuf[high, j, z] = total.astype(BF16)

    hsend = [
        remote(agbuf.at[high, j], agbuf.at[high, j], hs.at[j], hr.at[j], across)
        for j in range(NJ)
    ]

    def swap(j):
        for c in gsend[j]:
            c.wait_recv()
        hsend[j].start()

    mirror = remote(poly.at[:, pl.ds(S, S)], mbuf, ms.at[0], mr.at[0], mirror_to)

    def place(j):
        remote(
            agbuf.at[1 - high, j], agbuf.at[1 - high, j], hs.at[j], hr.at[j], across
        ).wait_recv()
        for half in range(2):
            for p in range(8):
                at_row = half * HB + p % 2 * PR
                at_col = j * S + p // 2 * PC
                poly[at_row : at_row + PR, at_col : at_col + PC] = agbuf[half, j, p]
        if j == 1:
            mirror.start()

    relay(0)
    relay(1)
    relay(2)

    @pl.when(core == 1)
    def _():
        for k in range(2):
            remote(
                x_ref, panel.at[k, pl.ds(NX * S, B)], ls.at[0], lr.at[k],
                at(low_=1 - low, core_=1),
            ).wait_recv()

    make(0)
    done([0, 2])
    make(1)
    scatter(0)
    relay(4)
    relay(5)
    done([4, 5])
    make(2)
    scatter(1)
    relay(3)
    spread(0)
    scatter(2)
    swap(0)
    spread(1)
    place(0)
    swap(1)
    spread(2)
    place(1)
    swap(2)
    done([1, 3])

    def send_partial(n, q):
        one = remote(
            part.at[n, q, 1], rbuf.at[n, q, core], ps.at[n, q, 1], pr.at[n, q, core],
            at(low_=other_low, core_=1),
        )
        one.start()

        @pl.when(core == 1)
        def _():
            remote(
                part.at[n, q, 0], rbuf.at[n, q, 1], ps.at[n, q, 0], pr.at[n, q, 1],
                at(low_=1 - low, core_=0),
            ).start()

    def reduced(n, q):
        remote(
            part.at[n, q, 1], rbuf.at[n, q, 1], ps.at[n, q, 1], pr.at[n, q, 1], twin
        ).wait_recv()

        @pl.when(core == 1)
        def _():
            remote(
                part.at[n, q, 0], rbuf.at[n, q, 0], ps.at[n, q, 0], pr.at[n, q, 0], twin
            ).wait_recv()

        @pl.when(core == 0)
        def _():
            rbuf[n, q, 0] = part[n, q, 0]

        return rbuf[n, q, 0].astype(F32) + rbuf[n, q, 1].astype(F32)

    def partial_close(n, q):
        remote(
            part.at[n, q, 1], rbuf.at[n, q, 1], ps.at[n, q, 1], pr.at[n, q, 1], twin
        ).wait_send()

        @pl.when(core == 1)
        def _():
            remote(
                part.at[n, q, 0], rbuf.at[n, q, 0], ps.at[n, q, 0], pr.at[n, q, 0], twin
            ).wait_send()

    def early(q, c):
        return jnp.dot(
            poly[:, 0 : 2 * S], panel[c, 0 : 2 * S, q * Q : (q + 1) * Q],
            preferred_element_type=F32,
        )

    for q in range(NQ):
        for c in range(2):
            yown[q, c] = early(q, c)
    place(2)
    mirror.wait_recv()
    turned = mbuf[...].astype(F32).T
    poly[:, 3 * S : 3 * S + B] = turned[0:B, :].astype(BF16)
    poly[:, 3 * S + B : 4 * S] = jnp.zeros((B, S - B), BF16)
    for q in range(NQ):
        for c in range(2):
            term = yown[q, c] + jnp.dot(
                poly[:, 2 * S : 4 * S], panel[c, 2 * S : 4 * S, q * Q : (q + 1) * Q],
                preferred_element_type=F32,
            )
            yown[q, c] = term
            part[0, q, c] = term.astype(BF16)
        send_partial(0, q)
    rings = []
    for q in range(NQ):
        ypanel[q, core, pl.ds(0, B)] = reduced(0, q).astype(BF16)

        def yslot(c, at_row, rows, q=q):
            return ypanel.at[q, c, pl.ds(at_row, rows)]

        rings.append(gather(ypanel.at[q, core, pl.ds(0, B)], yslot, 1 + q))
        rings[q][0]()
    for q in range(NQ):
        for k in range(6):
            rings[q][1](k)
    for q in range(NQ):
        rings[q][2](range(7))
        for c in range(2):
            term = jnp.dot(poly[...], ypanel[q, c], preferred_element_type=F32)
            part[1, q, c] = (2.0315 * term - 4.775 * yown[q, c]).astype(BF16)
        send_partial(1, q)
    scale = math.sqrt(N)
    for q in range(NQ):
        cols = slice(q * Q, (q + 1) * Q)
        total = 3.4445 * x_ref[:, cols].astype(F32) + reduced(1, q)
        out_ref[:, cols] = (total * scale).astype(BF16)

    close()
    other.wait_send()
    mirror.wait_send()
    for j in range(NJ):
        for c in [ysend[j], hsend[j]] + zsend[j] + gsend[j]:
            c.wait_send()
    for q in range(NQ):
        rings[q][3]()
        for n in range(2):
            partial_close(n, q)


def on_device(iterate):
    dma = pltpu.SemaphoreType.DMA
    return pl.pallas_call(
        kernel,
        out_shape=jax.ShapeDtypeStruct((B, W), BF16),
        in_specs=[pl.BlockSpec(memory_space=pltpu.VMEM)],
        out_specs=pl.BlockSpec(memory_space=pltpu.VMEM),
        scratch_shapes=[
            pltpu.VMEM((2, NX * S + B, W), BF16),
            pltpu.VMEM((NQ, 2, NX * S, Q), BF16),
            pltpu.VMEM((NJ, HB, S), BF16),
            pltpu.VMEM((NJ, HB, S), F32),
            pltpu.VMEM((NJ, HB, S), BF16),
            pltpu.VMEM((NJ, 8, PR, PC), BF16),
            pltpu.VMEM((NJ, 7, PR, PC), BF16),
            pltpu.VMEM((NJ, PR, PC), BF16),
            pltpu.VMEM((2, NJ, 8, PR, PC), BF16),
            pltpu.VMEM((B, NX * S), BF16),
            pltpu.VMEM((B, S), BF16),
            pltpu.VMEM((2, NQ, 2, B, Q), BF16),
            pltpu.VMEM((2, NQ, 2, B, Q), BF16),
            pltpu.VMEM((NQ, 2, B, Q), F32),
            dma,
            dma((1 + NQ, 6)), dma((1 + NQ, 6)),
            dma((1 + NQ, 7)), dma((1 + NQ, 7)),
            dma((1,)), dma((2,)),
            dma((NJ,)), dma((NJ,)),
            dma((NJ, 7)), dma((NJ, 7)),
            dma((NJ, 7)), dma((NJ, 7)),
            dma((NJ,)), dma((NJ,)),
            dma((1,)), dma((1,)),
            dma((2, NQ, 2)), dma((2, NQ, 2)),
        ],
        compiler_params=pltpu.CompilerParams(
            collective_id=0, has_side_effects=True, vmem_limit_bytes=56 * 2**20
        ),
    )(iterate)


def solution(mesh):
    in_specs = (P("row", "col"),)
    out_specs = P("row", "col")
    return jax.shard_map(
        on_device, mesh=mesh, in_specs=in_specs, out_specs=out_specs, check_vma=False
    )
```

time: 136 us -> 117 us (0.86)
  the two profiles are of different devices: /device:TPU:1 before, /device:TPU:128 now
where the time goes in v2:
time: 117 us
  Pallas kernels  115 us (98%)
  local copies, waits for them, and re-layouts  1.82 us (2%)
    pallas_call x1, Pallas kernels, on_device(): pl.pallas_call(kernel, out_shape=jax.ShapeDtypeStruct((B, W), BF16), in_s...  115 us

profile of v2, /device:TPU:128, one launch (start us, length us, event | category | flops | bytes accessed | tf_op | source)
XLA Modules:
  0.0 116.8 jit_solution(10801669736690732318)
XLA Ops:
  0.0 115.0 %shard_map.17 = bf16[448,512]{1,0:T(8,128)(2,1)} custom-call(bf16[448,512]{1,0:T(8,128)(2,1)} %x_ref.1), custom_call_target="tpu_custom_call" | custom-call | tf_op jit(solution)/shard_map/pallas_call | solution.py:360
  115.0 1.8 %copy.3 = bf16[448,512]{1,0:T(8,128)(2,1)} copy(bf16[448,512]{1,0:T(8,128)(2,1)} %shard_map.17) | data formatting | bytes 917504

commit v3 on v2

--- a/solution.py
+++ b/solution.py
@@ -13,7 +13,7 @@
 S = 512
 NX = 4
 NJ = 3
-NQ = 2
+NQ = 4
 Q = W // NQ
 HB = B // 2
 PR = HB // 2
@@ -25,7 +25,7 @@
 
 
 def kernel(
-    x_ref, out_ref, panel, ypanel, tsend, town, ybuf, zsrc, zbuf, gsh, agbuf, poly, mbuf,
+    x_ref, out_ref, panel, ypanel, tsend, town, ybuf, zsrc, zbuf, gsh, agbuf, poly, mfull,
     part, rbuf, yown, loc_sem, xs, xr, cs, cr, ls, lr, ys, yr, zs, zr, gs, gr, hs, hr,
     ms, mr, ps, pr,
 ):
@@ -101,15 +101,13 @@
 
         def start():
             cross[6].start()
-            for k in range(3):
-                direct[k].start()
+            for c in direct:
+                c.start()
 
         def relay(k):
             moves[k].wait_recv()
             if k < 2:
                 passed[k].start()
-            if k == 1:
-                direct[3].start()
             cross[k].start()
 
         def done(ks):
@@ -127,10 +125,16 @@
 
     start, relay, done, close = gather(x_ref, xslot, 0)
     start()
-    other = remote(
-        x_ref, panel.at[core, pl.ds(NX * S, B)], ls.at[0], lr.at[core], at(low_=1 - low, core_=1)
-    )
-    other.start()
+    def other(k, c):
+        half = (1 - high) if k == 0 else high
+        rows = pl.multiple_of(half * HB, 32)
+        return remote(
+            x_ref.at[pl.ds(rows, HB)], panel.at[c, pl.ds(NX * S + rows, HB)], ls.at[k],
+            lr.at[k, c], at(low_=1 - low, core_=1),
+        )
+
+    for k in range(2):
+        other(k, core).start()
     keep = pltpu.make_async_copy(x_ref, panel.at[core, pl.ds(0, B)], loc_sem)
     keep.start()
     keep.wait()
@@ -150,9 +154,11 @@
 
     ysend = [remote(tsend.at[j], ybuf.at[j], ys.at[j], yr.at[j], across) for j in range(NJ)]
 
-    def make(j):
+    def make_sent(j):
         tsend[j] = gram(1 - high, j).astype(BF16)
         ysend[j].start()
+
+    def make_kept(j):
         town[j] = gram(high, j)
 
     zsend = [
@@ -175,16 +181,21 @@
         for c in zsend[j]:
             c.start()
 
-    gsend = [
+    def over_z(src, j, origin, d, to):
+        dst = agbuf.at[high, j, origin % 8]
+        return remote(src, dst, gs.at[j, d - 1], gr.at[j, d - 1], at(z_=to % 8))
+
+    gsend = [[over_z(gsh.at[j], j, z, d, z + d) for d in (1, 7, 2, 6)] for j in range(NX)]
+    gpass = [
         [
-            remote(
-                gsh.at[j], agbuf.at[high, j, z], gs.at[j, d - 1], gr.at[j, d - 1],
-                at(z_=(z + d) % 8),
-            )
-            for d in (1, 7, 2, 6, 3, 5, 4)
+            over_z(agbuf.at[high, j, o % 8], j, o, d, to)
+            for o, d, to in ((z + 6, 3, z + 1), (z + 6, 4, z + 2), (z + 2, 5, z + 7))
         ]
-        for j in range(NJ)
+        for j in range(NX)
     ]
+
+    def arrived(j, d):
+        over_z(gsh.at[j], j, z + 8 - d, d, z + 1).wait_recv()
 
     def spread(j):
         total = zsrc[j, z].astype(F32)
@@ -195,19 +206,34 @@
         gsh[j] = total.astype(BF16)
         for c in gsend[j]:
             c.start()
+        if j == 1:
+            mirror.start()
         agbuf[high, j, z] = total.astype(BF16)
+
+    def forward(j):
+        arrived(j, 2)
+        gpass[j][0].start()
+        gpass[j][1].start()
+        arrived(j, 6)
+        gpass[j][2].start()
 
     hsend = [
         remote(agbuf.at[high, j], agbuf.at[high, j], hs.at[j], hr.at[j], across)
-        for j in range(NJ)
+        for j in range(NX)
     ]
 
     def swap(j):
-        for c in gsend[j]:
-            c.wait_recv()
+        for d in (1, 7, 3, 5, 4):
+            arrived(j, d)
         hsend[j].start()
 
-    mirror = remote(poly.at[:, pl.ds(S, S)], mbuf, ms.at[0], mr.at[0], mirror_to)
+    mirror = remote(gsh.at[1], gsh.at[3], ms.at[0], mr.at[0], mirror_to)
+
+    def reflect():
+        mirror.wait_recv()
+        for c in gsend[3]:
+            c.start()
+        agbuf[high, 3, z] = gsh[3]
 
     def place(j):
         remote(
@@ -216,42 +242,91 @@
         for half in range(2):
             for p in range(8):
                 at_row = half * HB + p % 2 * PR
-                at_col = j * S + p // 2 * PC
-                poly[at_row : at_row + PR, at_col : at_col + PC] = agbuf[half, j, p]
-        if j == 1:
-            mirror.start()
-
-    relay(0)
-    relay(1)
-    relay(2)
+                at_col = p // 2 * PC
+                if j == 3:
+                    mfull[at_row : at_row + PR, at_col : at_col + PC] = agbuf[half, j, p].astype(F32)
+                else:
+                    at_col += j * S
+                    poly[at_row : at_row + PR, at_col : at_col + PC] = agbuf[half, j, p]
+        if j == 3:
+            turned = mfull[...].T
+            poly[:, 3 * S : 3 * S + B] = turned[0:B, :].astype(BF16)
+            poly[:, 3 * S + B : 4 * S] = jnp.zeros((B, S - B), BF16)
+
+    def wait_other(k):
+        for c in range(2):
+            other(k, c).wait_recv()
+
+    @pl.when(core == 0)
+    def _():
+        make_sent(0)
+        make_kept(0)
+        relay(0)
+        relay(1)
+        scatter(0)
+        relay(2)
+        done([0, 2])
+        make_sent(1)
+        make_kept(1)
+        relay(3)
+        relay(5)
+        relay(4)
+        done([4, 5])
+        make_sent(2)
+        make_kept(2)
+        spread(0)
+        scatter(1)
+        forward(0)
+        swap(0)
+        scatter(2)
+        spread(1)
+        place(0)
+        forward(1)
+        reflect()
+        spread(2)
+        swap(1)
+        forward(3)
+        forward(2)
+        place(1)
+        swap(3)
+        swap(2)
 
     @pl.when(core == 1)
     def _():
-        for k in range(2):
-            remote(
-                x_ref, panel.at[k, pl.ds(NX * S, B)], ls.at[0], lr.at[k],
-                at(low_=1 - low, core_=1),
-            ).wait_recv()
-
-    make(0)
-    done([0, 2])
-    make(1)
-    scatter(0)
-    relay(4)
-    relay(5)
-    done([4, 5])
-    make(2)
-    scatter(1)
-    relay(3)
-    spread(0)
-    scatter(2)
-    swap(0)
-    spread(1)
-    place(0)
-    swap(1)
-    spread(2)
-    place(1)
-    swap(2)
+        relay(0)
+        relay(1)
+        wait_other(0)
+        make_sent(0)
+        relay(2)
+        done([0, 2])
+        make_sent(1)
+        relay(3)
+        wait_other(1)
+        make_kept(0)
+        scatter(0)
+        relay(5)
+        make_kept(1)
+        relay(4)
+        done([4, 5])
+        make_sent(2)
+        make_kept(2)
+        scatter(1)
+        spread(0)
+        forward(0)
+        scatter(2)
+        spread(1)
+        swap(0)
+        forward(1)
+        reflect()
+        spread(2)
+        swap(1)
+        forward(3)
+        forward(2)
+        place(0)
+        place(1)
+        swap(3)
+        swap(2)
+
     done([1, 3])
 
     def send_partial(n, q):
@@ -296,47 +371,53 @@
                 part.at[n, q, 0], rbuf.at[n, q, 0], ps.at[n, q, 0], pr.at[n, q, 0], twin
             ).wait_send()
 
-    def early(q, c):
-        return jnp.dot(
-            poly[:, 0 : 2 * S], panel[c, 0 : 2 * S, q * Q : (q + 1) * Q],
-            preferred_element_type=F32,
+    def both(q, rows):
+        cols = slice(q * Q, (q + 1) * Q)
+        return jnp.concatenate([panel[0, rows, cols], panel[1, rows, cols]], axis=1)
+
+    for q in range(NQ):
+        yown[q] = jnp.dot(
+            poly[:, 0 : 2 * S], both(q, slice(0, 2 * S)), preferred_element_type=F32
         )
-
+    place(3)
+    place(2)
     for q in range(NQ):
+        term = yown[q] + jnp.dot(
+            poly[:, 2 * S : 4 * S], both(q, slice(2 * S, 4 * S)), preferred_element_type=F32
+        )
+        yown[q] = term
         for c in range(2):
-            yown[q, c] = early(q, c)
-    place(2)
-    mirror.wait_recv()
-    turned = mbuf[...].astype(F32).T
-    poly[:, 3 * S : 3 * S + B] = turned[0:B, :].astype(BF16)
-    poly[:, 3 * S + B : 4 * S] = jnp.zeros((B, S - B), BF16)
-    for q in range(NQ):
-        for c in range(2):
-            term = yown[q, c] + jnp.dot(
-                poly[:, 2 * S : 4 * S], panel[c, 2 * S : 4 * S, q * Q : (q + 1) * Q],
-                preferred_element_type=F32,
-            )
-            yown[q, c] = term
-            part[0, q, c] = term.astype(BF16)
+            part[0, q, c] = term[:, c * Q : (c + 1) * Q].astype(BF16)
         send_partial(0, q)
     rings = []
-    for q in range(NQ):
+
+    def begin(q):
         ypanel[q, core, pl.ds(0, B)] = reduced(0, q).astype(BF16)
 
-        def yslot(c, at_row, rows, q=q):
+        def yslot(c, at_row, rows):
             return ypanel.at[q, c, pl.ds(at_row, rows)]
 
         rings.append(gather(ypanel.at[q, core, pl.ds(0, B)], yslot, 1 + q))
         rings[q][0]()
-    for q in range(NQ):
-        for k in range(6):
-            rings[q][1](k)
-    for q in range(NQ):
+
+    def finish(q):
         rings[q][2](range(7))
+        both_y = jnp.concatenate([ypanel[q, 0], ypanel[q, 1]], axis=1)
+        term = jnp.dot(poly[...], both_y, preferred_element_type=F32)
+        term = 2.0315 * term - 4.775 * yown[q]
         for c in range(2):
-            term = jnp.dot(poly[...], ypanel[q, c], preferred_element_type=F32)
-            part[1, q, c] = (2.0315 * term - 4.775 * yown[q, c]).astype(BF16)
+            part[1, q, c] = term[:, c * Q : (c + 1) * Q].astype(BF16)
         send_partial(1, q)
+
+    for t in range(NQ + 3):
+        if t < NQ:
+            begin(t)
+        for back, ks in ((1, (0, 1)), (2, (2, 3)), (3, (4, 5))):
+            if 0 <= t - back < NQ:
+                for k in ks:
+                    rings[t - back][1](k)
+        if t >= 3:
+            finish(t - 3)
     scale = math.sqrt(N)
     for q in range(NQ):
         cols = slice(q * Q, (q + 1) * Q)
@@ -344,10 +425,14 @@
         out_ref[:, cols] = (total * scale).astype(BF16)
 
     close()
-    other.wait_send()
+    for k in range(2):
+        other(k, core).wait_send()
     mirror.wait_send()
     for j in range(NJ):
-        for c in [ysend[j], hsend[j]] + zsend[j] + gsend[j]:
+        for c in [ysend[j]] + zsend[j]:
+            c.wait_send()
+    for j in range(NX):
+        for c in [hsend[j]] + gsend[j] + gpass[j]:
             c.wait_send()
     for q in range(NQ):
         rings[q][3]()
@@ -370,21 +455,21 @@
             pltpu.VMEM((NJ, HB, S), BF16),
             pltpu.VMEM((NJ, 8, PR, PC), BF16),
             pltpu.VMEM((NJ, 7, PR, PC), BF16),
-            pltpu.VMEM((NJ, PR, PC), BF16),
-            pltpu.VMEM((2, NJ, 8, PR, PC), BF16),
+            pltpu.VMEM((NX, PR, PC), BF16),
+            pltpu.VMEM((2, NX, 8, PR, PC), BF16),
             pltpu.VMEM((B, NX * S), BF16),
-            pltpu.VMEM((B, S), BF16),
+            pltpu.VMEM((B, S), F32),
             pltpu.VMEM((2, NQ, 2, B, Q), BF16),
             pltpu.VMEM((2, NQ, 2, B, Q), BF16),
-            pltpu.VMEM((NQ, 2, B, Q), F32),
+            pltpu.VMEM((NQ, B, 2 * Q), F32),
             dma,
             dma((1 + NQ, 6)), dma((1 + NQ, 6)),
             dma((1 + NQ, 7)), dma((1 + NQ, 7)),
-            dma((1,)), dma((2,)),
+            dma((2,)), dma((2, 2)),
             dma((NJ,)), dma((NJ,)),
             dma((NJ, 7)), dma((NJ, 7)),
-            dma((NJ, 7)), dma((NJ, 7)),
-            dma((NJ,)), dma((NJ,)),
+            dma((NX, 7)), dma((NX, 7)),
+            dma((NX,)), dma((NX,)),
             dma((1,)), dma((1,)),
             dma((2, NQ, 2)), dma((2, NQ, 2)),
         ],

time: 117 us -> 115 us (0.983)
  the two profiles are of different devices: /device:TPU:128 before, /device:TPU:1 now
where the time goes in v3:
time: 115 us
  Pallas kernels  113 us (98%)
  local copies, waits for them, and re-layouts  1.82 us (2%)
    pallas_call x1, Pallas kernels, on_device(): pl.pallas_call(kernel, out_shape=jax.ShapeDtypeStruct((B, W), BF16), in_s...  113 us

profile of v3, /device:TPU:1, one launch (start us, length us, event | category | flops | bytes accessed | tf_op | source)
XLA Modules:
  0.0 115.2 jit_solution(7506407681273299479)
XLA Ops:
  0.0 113.4 %shard_map.17 = bf16[448,512]{1,0:T(8,128)(2,1)} custom-call(bf16[448,512]{1,0:T(8,128)(2,1)} %x_ref.1), custom_call_target="tpu_custom_call" | custom-call | tf_op jit(solution)/shard_map/pallas_call | solution.py:445
  113.4 1.8 %copy.3 = bf16[448,512]{1,0:T(8,128)(2,1)} copy(bf16[448,512]{1,0:T(8,128)(2,1)} %shard_map.17) | data formatting | bytes 917504

commit v4 on v3

--- a/solution.py
+++ b/solution.py
@@ -185,13 +185,8 @@
         dst = agbuf.at[high, j, origin % 8]
         return remote(src, dst, gs.at[j, d - 1], gr.at[j, d - 1], at(z_=to % 8))
 
-    gsend = [[over_z(gsh.at[j], j, z, d, z + d) for d in (1, 7, 2, 6)] for j in range(NX)]
-    gpass = [
-        [
-            over_z(agbuf.at[high, j, o % 8], j, o, d, to)
-            for o, d, to in ((z + 6, 3, z + 1), (z + 6, 4, z + 2), (z + 2, 5, z + 7))
-        ]
-        for j in range(NX)
+    gsend = [
+        [over_z(gsh.at[j], j, z, d, z + d) for d in (1, 7, 2, 6, 3, 5, 4)] for j in range(NX)
     ]
 
     def arrived(j, d):
@@ -210,20 +205,13 @@
             mirror.start()
         agbuf[high, j, z] = total.astype(BF16)
 
-    def forward(j):
-        arrived(j, 2)
-        gpass[j][0].start()
-        gpass[j][1].start()
-        arrived(j, 6)
-        gpass[j][2].start()
-
     hsend = [
         remote(agbuf.at[high, j], agbuf.at[high, j], hs.at[j], hr.at[j], across)
         for j in range(NX)
     ]
 
     def swap(j):
-        for d in (1, 7, 3, 5, 4):
+        for d in range(1, 8):
             arrived(j, d)
         hsend[j].start()
 
@@ -276,20 +264,16 @@
         make_kept(2)
         spread(0)
         scatter(1)
-        forward(0)
         swap(0)
         scatter(2)
         spread(1)
-        place(0)
-        forward(1)
         reflect()
         spread(2)
         swap(1)
-        forward(3)
-        forward(2)
+        swap(3)
+        place(0)
+        swap(2)
         place(1)
-        swap(3)
-        swap(2)
 
     @pl.when(core == 1)
     def _():
@@ -312,20 +296,16 @@
         make_kept(2)
         scatter(1)
         spread(0)
-        forward(0)
         scatter(2)
         spread(1)
+        reflect()
         swap(0)
-        forward(1)
-        reflect()
         spread(2)
         swap(1)
-        forward(3)
-        forward(2)
+        swap(3)
         place(0)
+        swap(2)
         place(1)
-        swap(3)
-        swap(2)
 
     done([1, 3])
 
@@ -432,7 +412,7 @@
         for c in [ysend[j]] + zsend[j]:
             c.wait_send()
     for j in range(NX):
-        for c in [hsend[j]] + gsend[j] + gpass[j]:
+        for c in [hsend[j]] + gsend[j]:
             c.wait_send()
     for q in range(NQ):
         rings[q][3]()

time: 115 us -> 111 us (0.965); the launches traced: 115 us -> 109 us
  Pallas kernels: 113 us -> 107 us
    pallas_call x1, Pallas kernels: 113 us -> 107 us  [on_device(): pl.pallas_call(kernel, out_shape=jax.ShapeDtypeStruct((B, W), BF16), in_s...]
where the time goes in v4:
time: 111 us; the launch traced here: 109 us
  Pallas kernels  107 us (96%)
  local copies, waits for them, and re-layouts  1.82 us (2%)
    pallas_call x1, Pallas kernels, on_device(): pl.pallas_call(kernel, out_shape=jax.ShapeDtypeStruct((B, W), BF16), in_s...  107 us

profile of v4, /device:TPU:1, one launch (start us, length us, event | category | flops | bytes accessed | tf_op | source)
XLA Modules:
  0.0 109.2 jit_solution(14924835305336041728)
XLA Ops:
  0.0 107.3 %shard_map.17 = bf16[448,512]{1,0:T(8,128)(2,1)} custom-call(bf16[448,512]{1,0:T(8,128)(2,1)} %x_ref.1), custom_call_target="tpu_custom_call" | custom-call | tf_op jit(solution)/shard_map/pallas_call | solution.py:425
  107.3 1.8 %copy.3 = bf16[448,512]{1,0:T(8,128)(2,1)} copy(bf16[448,512]{1,0:T(8,128)(2,1)} %shard_map.17) | data formatting | bytes 917504

commit v5 on v4

--- a/solution.py
+++ b/solution.py
@@ -204,16 +204,23 @@
         if j == 1:
             mirror.start()
         agbuf[high, j, z] = total.astype(BF16)
+        hsend[j][0].start()
 
     hsend = [
-        remote(agbuf.at[high, j], agbuf.at[high, j], hs.at[j], hr.at[j], across)
+        [
+            remote(
+                agbuf.at[high, j, (z + 8 - d) % 8], agbuf.at[high, j, (z + 8 - d) % 8],
+                hs.at[j, d], hr.at[j, d], across,
+            )
+            for d in range(8)
+        ]
         for j in range(NX)
     ]
 
     def swap(j):
-        for d in range(1, 8):
+        for d in (1, 7, 2, 6, 3, 5, 4):
             arrived(j, d)
-        hsend[j].start()
+            hsend[j][d].start()
 
     mirror = remote(gsh.at[1], gsh.at[3], ms.at[0], mr.at[0], mirror_to)
 
@@ -222,11 +229,11 @@
         for c in gsend[3]:
             c.start()
         agbuf[high, 3, z] = gsh[3]
+        hsend[3][0].start()
 
     def place(j):
-        remote(
-            agbuf.at[1 - high, j], agbuf.at[1 - high, j], hs.at[j], hr.at[j], across
-        ).wait_recv()
+        for c in hsend[j]:
+            c.wait_recv()
         for half in range(2):
             for p in range(8):
                 at_row = half * HB + p % 2 * PR
@@ -360,10 +367,14 @@
             poly[:, 0 : 2 * S], both(q, slice(0, 2 * S)), preferred_element_type=F32
         )
     place(3)
+    for q in range(NQ):
+        yown[q] += jnp.dot(
+            poly[:, 3 * S : 4 * S], both(q, slice(3 * S, 4 * S)), preferred_element_type=F32
+        )
     place(2)
     for q in range(NQ):
         term = yown[q] + jnp.dot(
-            poly[:, 2 * S : 4 * S], both(q, slice(2 * S, 4 * S)), preferred_element_type=F32
+            poly[:, 2 * S : 3 * S], both(q, slice(2 * S, 3 * S)), preferred_element_type=F32
         )
         yown[q] = term
         for c in range(2):
@@ -412,7 +423,7 @@
         for c in [ysend[j]] + zsend[j]:
             c.wait_send()
     for j in range(NX):
-        for c in [hsend[j]] + gsend[j]:
+        for c in hsend[j] + gsend[j]:
             c.wait_send()
     for q in range(NQ):
         rings[q][3]()
@@ -449,7 +460,7 @@
             dma((NJ,)), dma((NJ,)),
             dma((NJ, 7)), dma((NJ, 7)),
             dma((NX, 7)), dma((NX, 7)),
-            dma((NX,)), dma((NX,)),
+            dma((NX, 8)), dma((NX, 8)),
             dma((1,)), dma((1,)),
             dma((2, NQ, 2)), dma((2, NQ, 2)),
         ],

time: 111 us -> 107 us (0.964); the launches traced: 109 us -> 106 us
  Pallas kernels: 107 us -> 105 us
    pallas_call x1, Pallas kernels: 107 us -> 105 us  [on_device(): pl.pallas_call(kernel, out_shape=jax.ShapeDtypeStruct((B, W), BF16), in_s...]
where the time goes in v5:
time: 107 us; the launch traced here: 106 us
  Pallas kernels  105 us (98%)
  local copies, waits for them, and re-layouts  1.82 us (2%)
    pallas_call x1, Pallas kernels, on_device(): pl.pallas_call(kernel, out_shape=jax.ShapeDtypeStruct((B, W), BF16), in_s...  105 us

profile of v5, /device:TPU:1, one launch (start us, length us, event | category | flops | bytes accessed | tf_op | source)
XLA Modules:
  0.0 106.4 jit_solution(9395708448607619294)
XLA Ops:
  0.0 104.6 %shard_map.17 = bf16[448,512]{1,0:T(8,128)(2,1)} custom-call(bf16[448,512]{1,0:T(8,128)(2,1)} %x_ref.1), custom_call_target="tpu_custom_call" | custom-call | tf_op jit(solution)/shard_map/pallas_call | solution.py:436
  104.6 1.8 %copy.3 = bf16[448,512]{1,0:T(8,128)(2,1)} copy(bf16[448,512]{1,0:T(8,128)(2,1)} %shard_map.17) | data formatting | bytes 917504

commit v6 on v5

--- a/solution.py
+++ b/solution.py
@@ -167,7 +167,7 @@
                 zsrc.at[j, (z + d) % 8], zbuf.at[j, d - 1], zs.at[j, d - 1], zr.at[j, d - 1],
                 at(z_=(z + d) % 8),
             )
-            for d in (1, 7, 2, 6, 3, 5, 4)
+            for d in (4, 3, 5, 2, 6, 1, 7)
         ]
         for j in range(NJ)
     ]
@@ -186,7 +186,7 @@
         return remote(src, dst, gs.at[j, d - 1], gr.at[j, d - 1], at(z_=to % 8))
 
     gsend = [
-        [over_z(gsh.at[j], j, z, d, z + d) for d in (1, 7, 2, 6, 3, 5, 4)] for j in range(NX)
+        [over_z(gsh.at[j], j, z, d, z + d) for d in (4, 3, 5, 2, 6, 1, 7)] for j in range(NX)
     ]
 
     def arrived(j, d):

time: 107 us -> 109 us (1.019)
    pallas_call x1, Pallas kernels: 105 us -> 106 us  [on_device(): pl.pallas_call(kernel, out_shape=jax.ShapeDtypeStruct((B, W), BF16), in_s...]
where the time goes in v6:
time: 109 us; the launch traced here: 108 us
  Pallas kernels  106 us (97%)
  local copies, waits for them, and re-layouts  1.82 us (2%)
    pallas_call x1, Pallas kernels, on_device(): pl.pallas_call(kernel, out_shape=jax.ShapeDtypeStruct((B, W), BF16), in_s...  106 us

profile of v6, /device:TPU:1, one launch (start us, length us, event | category | flops | bytes accessed | tf_op | source)
XLA Modules:
  0.0 108.3 jit_solution(10173553398406167545)
XLA Ops:
  0.0 106.4 %shard_map.17 = bf16[448,512]{1,0:T(8,128)(2,1)} custom-call(bf16[448,512]{1,0:T(8,128)(2,1)} %x_ref.1), custom_call_target="tpu_custom_call" | custom-call | tf_op jit(solution)/shard_map/pallas_call | solution.py:436
  106.4 1.8 %copy.3 = bf16[448,512]{1,0:T(8,128)(2,1)} copy(bf16[448,512]{1,0:T(8,128)(2,1)} %shard_map.17) | data formatting | bytes 917504
